TPU v7x, 32 devices: a whole 2x2x4 slice. The times are simulated.
32 devices in a mesh: section: 8 (over y, x, core), dp: 4 (over z).
Axes of the slice: x: 2, y: 2, z: 4, core: 2. Of those that a mesh axis runs over, the one named last changes fastest.
Arguments:
- images: bfloat16 [12, 256, 512], P(None, 'dp'), may hold values from -6 to 6
- cotangent: bfloat16 [12, 256, 512], P(None, 'dp'), may hold values from -6 to 6
- w_in: bfloat16 [8, 4, 512, 512], P('section', None, 'dp'), may hold values from -0.25 to 0.25
- w_out: bfloat16 [8, 4, 512, 512], P('section', None, 'dp'), may hold values from -0.0625 to 0.0625
Outputs:
- new_in: float32 [8, 4, 512, 512], P('section', None, 'dp')
- new_out: float32 [8, 4, 512, 512], P('section', None, 'dp')
All inputs are finite; a program needn't handle non-finite values.
Results may differ from a plain program's by a relative error of at most 0.03.
Values may be sent and summed in bfloat16 or wider, within the bound.
A program may use at most 128 MiB of HBM per device.

v0:
```python
import math

import jax
import jax.numpy as jnp
from jax import lax
from jax.sharding import PartitionSpec as P


def shifted(value, axis, steps):
    count = lax.axis_size(axis)
    initial, last = (max(0, -steps), min(count, count - steps))
    return lax.ppermute(value, axis, [(source, source + steps) for source in range(initial, last)])


def per_device(images, cotangent, w_in, w_out):
    sections = lax.axis_size("section")
    place = lax.axis_index("section")
    groups = lax.axis_size("dp")
    full_in, full_out = (
        lax.all_gather(w_in, "dp", axis=2, tiled=True),
        lax.all_gather(w_out, "dp", axis=2, tiled=True),
    )
    first = full_in[0]
    second = full_out[0]
    micro, rows, width = images.shape
    layers = first.shape[0]
    ticks = micro + sections - 1
    zero_rows = jnp.zeros((rows, width), jnp.bfloat16)
    zero_stack = jnp.zeros((layers, rows, width), jnp.bfloat16)
    contract = (((1,), (1,)), ((), ()))

    def forward_section(value):
        inputs = []
        for layer in range(layers):
            inputs.append(value)
            pre = jnp.dot(value, first[layer], preferred_element_type=jnp.float32)
            hidden = (pre * jax.nn.sigmoid(pre)).astype(jnp.bfloat16)
            value = (
                value.astype(jnp.float32)
                + jnp.dot(hidden, second[layer], preferred_element_type=jnp.float32)
            ).astype(jnp.bfloat16)
        return (value, jnp.stack(inputs))

    def backward_section(inputs, grad):
        hiddens, dpres, grads = ([], [], [])
        for layer in reversed(range(layers)):
            value = inputs[layer]
            pre = jnp.dot(value, first[layer], preferred_element_type=jnp.float32)
            sig = jax.nn.sigmoid(pre)
            hiddens.append((pre * sig).astype(jnp.bfloat16))
            grads.append(grad)
            dhidden = lax.dot_general(
                grad, second[layer], contract, preferred_element_type=jnp.float32
            )
            dpre = (dhidden * (sig * (1.0 + pre * (1.0 - sig)))).astype(jnp.bfloat16)
            dpres.append(dpre)
            grad = (
                grad.astype(jnp.float32)
                + lax.dot_general(dpre, first[layer], contract, preferred_element_type=jnp.float32)
            ).astype(jnp.bfloat16)
        return (grad, jnp.stack(hiddens[::-1]), jnp.stack(dpres[::-1]), jnp.stack(grads[::-1]))

    def put(store, index, valid, fresh, axis_pos):
        old = lax.dynamic_index_in_dim(store, index, axis_pos, keepdims=False)
        return lax.dynamic_update_index_in_dim(store, jnp.where(valid, fresh, old), index, axis_pos)

    kept0 = jnp.zeros((layers, micro, rows, width), jnp.bfloat16)

    def forward_tick(carry, tick):
        incoming, kept = carry
        slot = tick - place
        valid = (slot >= 0) & (slot < micro)
        index = jnp.clip(slot, 0, micro - 1)
        fresh = lax.dynamic_index_in_dim(images, index, 0, keepdims=False)
        source = jnp.where(place == 0, fresh, incoming)
        output, inputs = lax.cond(
            valid, lambda: forward_section(source), lambda: (zero_rows, zero_stack)
        )
        kept = put(kept, index, valid, inputs, 1)
        passed = shifted(output, "section", 1)
        return ((passed, kept), None)

    (unused_in, kept), unused = lax.scan(
        forward_tick, (zero_rows, kept0), jnp.arange(ticks, dtype=jnp.int32)
    )

    def relay_step(tick, incoming):
        slot = tick - (sections - 1 - place)
        valid = (slot >= 0) & (slot < micro)
        index = jnp.clip(slot, 0, micro - 1)
        fresh = lax.dynamic_index_in_dim(cotangent, index, 0, keepdims=False)
        upstream = jnp.where(place == sections - 1, fresh, incoming)
        inputs = lax.dynamic_index_in_dim(kept, index, 1, keepdims=False)

        def run():
            back, hiddens, dpres, grads = backward_section(inputs, upstream)
            return (back, hiddens, dpres, grads)

        back, hiddens, dpres, grads = lax.cond(
            valid, run, lambda: (zero_rows, zero_stack, zero_stack, zero_stack)
        )
        passed = shifted(back, "section", -1)
        return (passed, valid, index, inputs, hiddens, dpres, grads)

    blank = jnp.zeros((layers, micro, rows, width), jnp.bfloat16)

    def backward_tick(carry, tick):
        incoming, hidden_all, dpre_all, grad_all = carry
        passed, valid, index, inputs, hiddens, dpres, grads = relay_step(tick, incoming)
        hidden_all = put(hidden_all, index, valid, hiddens, 1)
        dpre_all = put(dpre_all, index, valid, dpres, 1)
        grad_all = put(grad_all, index, valid, grads, 1)
        return ((passed, hidden_all, dpre_all, grad_all), None)

    (unused_back, hidden_all, dpre_all, grad_all), unused = lax.scan(
        backward_tick, (zero_rows, blank, blank, blank), jnp.arange(ticks, dtype=jnp.int32)
    )
    flat_inputs = kept.reshape(layers, micro * rows, width)
    flat_hidden = hidden_all.reshape(layers, micro * rows, width)
    flat_dpre = dpre_all.reshape(layers, micro * rows, width)
    flat_grad = grad_all.reshape(layers, micro * rows, width)
    grad_in = None
    grad_out = None
    grad_in = jnp.einsum("lrc,lrd->lcd", flat_inputs, flat_dpre, preferred_element_type=jnp.float32)
    grad_out = jnp.einsum(
        "lrc,lrd->lcd", flat_hidden, flat_grad, preferred_element_type=jnp.float32
    )
    share_in, share_out = (
        lax.psum_scatter(grad_in, "dp", scatter_dimension=1, tiled=True),
        lax.psum_scatter(grad_out, "dp", scatter_dimension=1, tiled=True),
    )
    rate = 0.1 / math.sqrt(micro * rows * groups)
    new_in = w_in.astype(jnp.float32) - rate * share_in[None]
    new_out = w_out.astype(jnp.float32) - rate * share_out[None]
    return (new_in, new_out)


def solution(mesh):
    in_specs = (
        P(None, "dp", None),
        P(None, "dp", None),
        P("section", None, "dp", None),
        P("section", None, "dp", None),
    )
    out_specs = (P("section", None, "dp", None), P("section", None, "dp", None))
    return jax.shard_map(
        per_device, mesh=mesh, in_specs=in_specs, out_specs=out_specs, check_vma=False
    )
```

profile of v0, /device:TPU:8, one launch (start us, length us, event | category | flops | bytes accessed | tf_op | source)
XLA Modules:
  0.0 828.3 jit_solution(466928142596177172)
XLA Ops:
  8.7 46.4 %all-gather.3.cloned.1.call-done = bf16[1,4,512,512]{3,2,1,0:T(8,128)(2,1)} async-done(((bf16[1,4,128,512]{3,2,1,0:T(8,128)(2,1)}), bf16[1,4,512,512]{3,2,1,0:T(8,128)(2,1)}) %all-gather.3.cloned.1.call-update) | async-done | bytes 2097168 | tf_op jit(solution)/shard_map/all_gather | solution.py:20
  55.1 46.3 %all-gather.5.cloned.1.call-done = bf16[1,4,512,512]{3,2,1,0:T(8,128)(2,1)} async-done(((bf16[1,4,128,512]{3,2,1,0:T(8,128)(2,1)}), bf16[1,4,512,512]{3,2,1,0:T(8,128)(2,1)}) %all-gather.5.cloned.1.call-update) | async-done | bytes 2097168 | tf_op jit(solution)/shard_map/all_gather | solution.py:21
  101.3 2.0 broadcast.17.clone2
  103.3 235.0 %while.31 = (s32[]{:T(128)}, bf16[64,512]{1,0:T(8,128)(2,1)S(1)}, bf16[4,12,64,512]{3,2,1,0:T(8,128)(2,1)}, s32[19]{0:T(128)S(1)}, s32[]{:T(128)}, /*index=5*/pr...) while((s32[]{:T(128)}, bf16[64,512]{1,0:T(8,128)(2,1)S(1)}, ...), condition=%wide.region_3.4_spmd, body=%wide.region_0.3_spmd.sunk | while | flops 270106624 | bytes 7408441 | solution.py:83
  104.6 6.7 conditional.4
  104.6 1.4 fusion
  115.6 6.7 conditional.4
  126.7 6.7 conditional.4
  126.7 1.4 fusion
  133.4 1.9 collective-permute-start
  138.3 6.7 conditional.4
  145.0 3.8 collective-permute-start
  151.9 6.7 conditional.4
  151.9 1.5 fusion
  158.6 3.8 collective-permute-start
  165.4 6.7 conditional.4
  165.4 1.5 fusion
  172.1 3.9 collective-permute-start
  179.0 6.7 conditional.4
  179.0 1.4 fusion
  185.7 3.8 collective-permute-start
  192.5 6.7 conditional.4
  192.5 1.4 fusion
  199.2 3.8 collective-permute-start
  206.1 6.7 conditional.4
  212.7 3.9 collective-permute-start
  219.6 6.7 conditional.4
  226.3 3.8 collective-permute-start
  233.1 6.7 conditional.4
  239.8 3.8 collective-permute-start
  246.7 6.7 conditional.4
  253.4 3.8 collective-permute-start
  260.3 10.5 %collective-permute-start = (bf16[64,512]{1,0:T(8,128)(2,1)S(1)}, bf16[64,512]{1,0:T(8,128)(2,1)S(1)}, u32[]{:S(2)}, u32[]{:S(2)}) collective-permute-start(bf16[64,512]{1,0:T(8,128)(2,1)S(1)} %get-tuple-element.520), channel_id=1, source_target_pairs={{0,4},{4,8},{8,12},{12,16},{16,20},{20,24},{24,28},{1,5},{5,9},{9,... | collective-permute-start | bytes 196616 | tf_op jit(solution)/shard_map/while/body/eval_jaxpr/ppermute | solution.py:12
  273.8 3.8 collective-permute-start
  280.8 11.3 %collective-permute-start = (bf16[64,512]{1,0:T(8,128)(2,1)S(1)}, bf16[64,512]{1,0:T(8,128)(2,1)S(1)}, u32[]{:S(2)}, u32[]{:S(2)}) collective-permute-start(bf16[64,512]{1,0:T(8,128)(2,1)S(1)} %get-tuple-element.520), channel_id=1, source_target_pairs={{0,4},{4,8},{8,12},{12,16},{16,20},{20,24},{24,28},{1,5},{5,9},{9,... | collective-permute-start | bytes 196616 | tf_op jit(solution)/shard_map/while/body/eval_jaxpr/ppermute | solution.py:12
  295.2 4.7 collective-permute-start
  303.0 11.3 %collective-permute-start = (bf16[64,512]{1,0:T(8,128)(2,1)S(1)}, bf16[64,512]{1,0:T(8,128)(2,1)S(1)}, u32[]{:S(2)}, u32[]{:S(2)}) collective-permute-start(bf16[64,512]{1,0:T(8,128)(2,1)S(1)} %get-tuple-element.520), channel_id=1, source_target_pairs={{0,4},{4,8},{8,12},{12,16},{16,20},{20,24},{24,28},{1,5},{5,9},{9,... | collective-permute-start | bytes 196616 | tf_op jit(solution)/shard_map/while/body/eval_jaxpr/ppermute | solution.py:12
  317.5 4.7 collective-permute-start
  325.3 11.3 %collective-permute-start = (bf16[64,512]{1,0:T(8,128)(2,1)S(1)}, bf16[64,512]{1,0:T(8,128)(2,1)S(1)}, u32[]{:S(2)}, u32[]{:S(2)}) collective-permute-start(bf16[64,512]{1,0:T(8,128)(2,1)S(1)} %get-tuple-element.520), channel_id=1, source_target_pairs={{0,4},{4,8},{8,12},{12,16},{16,20},{20,24},{24,28},{1,5},{5,9},{9,... | collective-permute-start | bytes 196616 | tf_op jit(solution)/shard_map/while/body/eval_jaxpr/ppermute | solution.py:12
  338.4 2.1 broadcast.17.clone2.2
  340.5 2.1 broadcast.17.clone2.1
  342.6 2.1 broadcast.17.clone
  344.6 312.3 %while.32 = (s32[]{:T(128)}, bf16[64,512]{1,0:T(8,128)(2,1)S(1)}, bf16[4,12,64,512]{3,2,1,0:T(8,128)(2,1)}, bf16[4,12,64,512]{3,2,1,0:T(8,128)(2,1)}, bf16[4,12,...) while((s32[]{:T(128)}, bf16[64,512]{1,0:T(8,128)(2,1)S(1)}, ...), condition=%wide.region_7.8_spmd, body=%wide.region_4.7_spmd.sunk | while | flops 406487040 | bytes 24055228 | solution.py:115
  375.2 2.5 collective-permute-done.1
  400.9 56.2 %collective-permute-done.1 = bf16[64,512]{1,0:T(8,128)(2,1)S(1)} collective-permute-done((bf16[64,512]{1,0:T(8,128)(2,1)S(1)}, bf16[64,512]{1,0:T(8,128)(2,1)S(1)}, u32[]{:S(2)}, u32[]{:S(2)}) %collective-permute-start.1) | collective-permute-done | bytes 65568 | tf_op jit(solution)/shard_map/while/body/eval_jaxpr/ppermute | solution.py:12
  458.4 8.9 %conditional.5 = (bf16[64,512]{1,0:T(8,128)(2,1)S(1)}, bf16[4,64,512]{2,1,0:T(8,128)(2,1)S(1)}, bf16[4,64,512]{2,1,0:T(8,128)(2,1)S(1)}, bf16[4,64,512]{2,1,0:T(8,128)(2,1)S(1)}) conditional(s32[]{:T(128)} %convert_element_type.194, () %tuple.83, (pred[]{:T(512)}, bf16[12,64,512]{2,1,0:T(8,128)(2,1)}, s32[]{:T(128)}, bf16[64,512]{1,0:T(8,128)(2,1)S(1)}, ...), branch_computations={%region_5.5_spmd, %region_6.6_spmd} | conditional | flops 406093824 | bytes 19859568 | solution.py:99
  475.0 8.9 %conditional.5 = (bf16[64,512]{1,0:T(8,128)(2,1)S(1)}, bf16[4,64,512]{2,1,0:T(8,128)(2,1)S(1)}, bf16[4,64,512]{2,1,0:T(8,128)(2,1)S(1)}, bf16[4,64,512]{2,1,0:T(8,128)(2,1)S(1)}) conditional(s32[]{:T(128)} %convert_element_type.194, () %tuple.83, (pred[]{:T(512)}, bf16[12,64,512]{2,1,0:T(8,128)(2,1)}, s32[]{:T(128)}, bf16[64,512]{1,0:T(8,128)(2,1)S(1)}, ...), branch_computations={%region_5.5_spmd, %region_6.6_spmd} | conditional | flops 406093824 | bytes 19859568 | solution.py:99
  491.8 8.9 %conditional.5 = (bf16[64,512]{1,0:T(8,128)(2,1)S(1)}, bf16[4,64,512]{2,1,0:T(8,128)(2,1)S(1)}, bf16[4,64,512]{2,1,0:T(8,128)(2,1)S(1)}, bf16[4,64,512]{2,1,0:T(8,128)(2,1)S(1)}) conditional(s32[]{:T(128)} %convert_element_type.194, () %tuple.83, (pred[]{:T(512)}, bf16[12,64,512]{2,1,0:T(8,128)(2,1)}, s32[]{:T(128)}, bf16[64,512]{1,0:T(8,128)(2,1)S(1)}, ...), branch_computations={%region_5.5_spmd, %region_6.6_spmd} | conditional | flops 406093824 | bytes 19859568 | solution.py:99
  508.4 8.9 %conditional.5 = (bf16[64,512]{1,0:T(8,128)(2,1)S(1)}, bf16[4,64,512]{2,1,0:T(8,128)(2,1)S(1)}, bf16[4,64,512]{2,1,0:T(8,128)(2,1)S(1)}, bf16[4,64,512]{2,1,0:T(8,128)(2,1)S(1)}) conditional(s32[]{:T(128)} %convert_element_type.194, () %tuple.83, (pred[]{:T(512)}, bf16[12,64,512]{2,1,0:T(8,128)(2,1)}, s32[]{:T(128)}, bf16[64,512]{1,0:T(8,128)(2,1)S(1)}, ...), branch_computations={%region_5.5_spmd, %region_6.6_spmd} | conditional | flops 406093824 | bytes 19859568 | solution.py:99
  525.1 8.9 %conditional.5 = (bf16[64,512]{1,0:T(8,128)(2,1)S(1)}, bf16[4,64,512]{2,1,0:T(8,128)(2,1)S(1)}, bf16[4,64,512]{2,1,0:T(8,128)(2,1)S(1)}, bf16[4,64,512]{2,1,0:T(8,128)(2,1)S(1)}) conditional(s32[]{:T(128)} %convert_element_type.194, () %tuple.83, (pred[]{:T(512)}, bf16[12,64,512]{2,1,0:T(8,128)(2,1)}, s32[]{:T(128)}, bf16[64,512]{1,0:T(8,128)(2,1)S(1)}, ...), branch_computations={%region_5.5_spmd, %region_6.6_spmd} | conditional | flops 406093824 | bytes 19859568 | solution.py:99
  541.8 8.9 %conditional.5 = (bf16[64,512]{1,0:T(8,128)(2,1)S(1)}, bf16[4,64,512]{2,1,0:T(8,128)(2,1)S(1)}, bf16[4,64,512]{2,1,0:T(8,128)(2,1)S(1)}, bf16[4,64,512]{2,1,0:T(8,128)(2,1)S(1)}) conditional(s32[]{:T(128)} %convert_element_type.194, () %tuple.83, (pred[]{:T(512)}, bf16[12,64,512]{2,1,0:T(8,128)(2,1)}, s32[]{:T(128)}, bf16[64,512]{1,0:T(8,128)(2,1)S(1)}, ...), branch_computations={%region_5.5_spmd, %region_6.6_spmd} | conditional | flops 406093824 | bytes 19859568 | solution.py:99
  558.5 8.9 %conditional.5 = (bf16[64,512]{1,0:T(8,128)(2,1)S(1)}, bf16[4,64,512]{2,1,0:T(8,128)(2,1)S(1)}, bf16[4,64,512]{2,1,0:T(8,128)(2,1)S(1)}, bf16[4,64,512]{2,1,0:T(8,128)(2,1)S(1)}) conditional(s32[]{:T(128)} %convert_element_type.194, () %tuple.83, (pred[]{:T(512)}, bf16[12,64,512]{2,1,0:T(8,128)(2,1)}, s32[]{:T(128)}, bf16[64,512]{1,0:T(8,128)(2,1)S(1)}, ...), branch_computations={%region_5.5_spmd, %region_6.6_spmd} | conditional | flops 406093824 | bytes 19859568 | solution.py:99
  575.2 8.9 %conditional.5 = (bf16[64,512]{1,0:T(8,128)(2,1)S(1)}, bf16[4,64,512]{2,1,0:T(8,128)(2,1)S(1)}, bf16[4,64,512]{2,1,0:T(8,128)(2,1)S(1)}, bf16[4,64,512]{2,1,0:T(8,128)(2,1)S(1)}) conditional(s32[]{:T(128)} %convert_element_type.194, () %tuple.83, (pred[]{:T(512)}, bf16[12,64,512]{2,1,0:T(8,128)(2,1)}, s32[]{:T(128)}, bf16[64,512]{1,0:T(8,128)(2,1)S(1)}, ...), branch_computations={%region_5.5_spmd, %region_6.6_spmd} | conditional | flops 406093824 | bytes 19859568 | solution.py:99
  592.0 8.9 %conditional.5 = (bf16[64,512]{1,0:T(8,128)(2,1)S(1)}, bf16[4,64,512]{2,1,0:T(8,128)(2,1)S(1)}, bf16[4,64,512]{2,1,0:T(8,128)(2,1)S(1)}, bf16[4,64,512]{2,1,0:T(8,128)(2,1)S(1)}) conditional(s32[]{:T(128)} %convert_element_type.194, () %tuple.83, (pred[]{:T(512)}, bf16[12,64,512]{2,1,0:T(8,128)(2,1)}, s32[]{:T(128)}, bf16[64,512]{1,0:T(8,128)(2,1)S(1)}, ...), branch_computations={%region_5.5_spmd, %region_6.6_spmd} | conditional | flops 406093824 | bytes 19859568 | solution.py:99
  608.7 8.9 %conditional.5 = (bf16[64,512]{1,0:T(8,128)(2,1)S(1)}, bf16[4,64,512]{2,1,0:T(8,128)(2,1)S(1)}, bf16[4,64,512]{2,1,0:T(8,128)(2,1)S(1)}, bf16[4,64,512]{2,1,0:T(8,128)(2,1)S(1)}) conditional(s32[]{:T(128)} %convert_element_type.194, () %tuple.83, (pred[]{:T(512)}, bf16[12,64,512]{2,1,0:T(8,128)(2,1)}, s32[]{:T(128)}, bf16[64,512]{1,0:T(8,128)(2,1)S(1)}, ...), branch_computations={%region_5.5_spmd, %region_6.6_spmd} | conditional | flops 406093824 | bytes 19859568 | solution.py:99
  625.4 8.9 %conditional.5 = (bf16[64,512]{1,0:T(8,128)(2,1)S(1)}, bf16[4,64,512]{2,1,0:T(8,128)(2,1)S(1)}, bf16[4,64,512]{2,1,0:T(8,128)(2,1)S(1)}, bf16[4,64,512]{2,1,0:T(8,128)(2,1)S(1)}) conditional(s32[]{:T(128)} %convert_element_type.194, () %tuple.83, (pred[]{:T(512)}, bf16[12,64,512]{2,1,0:T(8,128)(2,1)}, s32[]{:T(128)}, bf16[64,512]{1,0:T(8,128)(2,1)S(1)}, ...), branch_computations={%region_5.5_spmd, %region_6.6_spmd} | conditional | flops 406093824 | bytes 19859568 | solution.py:99
  642.1 8.9 %conditional.5 = (bf16[64,512]{1,0:T(8,128)(2,1)S(1)}, bf16[4,64,512]{2,1,0:T(8,128)(2,1)S(1)}, bf16[4,64,512]{2,1,0:T(8,128)(2,1)S(1)}, bf16[4,64,512]{2,1,0:T(8,128)(2,1)S(1)}) conditional(s32[]{:T(128)} %convert_element_type.194, () %tuple.83, (pred[]{:T(512)}, bf16[12,64,512]{2,1,0:T(8,128)(2,1)}, s32[]{:T(128)}, bf16[64,512]{1,0:T(8,128)(2,1)S(1)}, ...), branch_computations={%region_5.5_spmd, %region_6.6_spmd} | conditional | flops 406093824 | bytes 19859568 | solution.py:99
  656.9 6.6 fusion.96
  663.6 1.8 copy-done.1
  665.4 5.7 fusion.95
  671.2 68.6 %reduce-scatter.5.cloned.1.call-done = f32[4,128,512]{2,1,0:T(8,128)} async-done(((f32[4,512,512]{2,1,0:T(8,128)}), f32[4,128,512]{2,1,0:T(8,128)}) %reduce-scatter.5.cloned.1.call-update) | async-done | bytes 1048592 | tf_op jit(solution)/shard_map/reduce_scatter | solution.py:130
  739.8 2.4 bitcast_subtract_fusion
  742.2 77.2 %reduce-scatter.3.cloned.1.call-done = f32[4,128,512]{2,1,0:T(8,128)} async-done(((f32[4,512,512]{2,1,0:T(8,128)}), f32[4,128,512]{2,1,0:T(8,128)}) %reduce-scatter.3.cloned.1.call-update) | async-done | bytes 1048592 | tf_op jit(solution)/shard_map/reduce_scatter | solution.py:129
  819.4 2.4 bitcast_subtract_fusion.1
  (597 shorter events, 360.8 us)
Async XLA Ops:
  7.2 47.9 %all-gather.3.cloned.1.call-start = ((), (), s32[]{:S(2)}) async-start(), calls=%async_computation.2 | async-start | bytes 2621440 | tf_op jit(solution)/shard_map/all_gather | solution.py:20
  7.9 93.4 %all-gather.5.cloned.1.call-start = ((), (), s32[]{:S(2)}) async-start(), calls=%async_computation.3 | async-start | bytes 2621440 | tf_op jit(solution)/shard_map/all_gather | solution.py:21
  8.6 731.1 %reduce-scatter.5.cloned.1.call-start = ((), (), s32[]{:S(2)}) async-start(), calls=%async_computation.5 | async-start | bytes 5242880 | tf_op jit(solution)/shard_map/reduce_scatter | solution.py:130
  55.1 48.3 %copy-start = (bf16[1,4,512,512]{3,2,1,0:T(8,128)(2,1)S(1)}, bf16[1,4,512,512]{3,2,1,0:T(8,128)(2,1)}, u32[]{:S(2)}) copy-start(bf16[1,4,512,512]{3,2,1,0:T(8,128)(2,1)} %all-gather.3.cloned.1.call-done) | copy-start | bytes 6291460
  111.3 3.1 collective-permute-start
  122.3 3.1 collective-permute-start
  133.4 3.7 collective-permute-start
  145.0 5.6 collective-permute-start
  158.6 5.5 collective-permute-start
  172.1 5.6 collective-permute-start
  185.7 5.6 collective-permute-start
  199.2 5.6 collective-permute-start
  212.7 5.6 collective-permute-start
  226.3 5.6 collective-permute-start
  239.8 5.6 collective-permute-start
  253.4 5.6 collective-permute-start
  260.3 12.2 %collective-permute-start = (bf16[64,512]{1,0:T(8,128)(2,1)S(1)}, bf16[64,512]{1,0:T(8,128)(2,1)S(1)}, u32[]{:S(2)}, u32[]{:S(2)}) collective-permute-start(bf16[64,512]{1,0:T(8,128)(2,1)S(1)} %get-tuple-element.520), channel_id=1, source_target_pairs={{0,4},{4,8},{8,12},{12,16},{16,20},{20,24},{24,28},{1,5},{5,9},{9,... | collective-permute-start | bytes 196616 | tf_op jit(solution)/shard_map/while/body/eval_jaxpr/ppermute | solution.py:12
  273.8 5.6 collective-permute-start
  280.8 13.1 %collective-permute-start = (bf16[64,512]{1,0:T(8,128)(2,1)S(1)}, bf16[64,512]{1,0:T(8,128)(2,1)S(1)}, u32[]{:S(2)}, u32[]{:S(2)}) collective-permute-start(bf16[64,512]{1,0:T(8,128)(2,1)S(1)} %get-tuple-element.520), channel_id=1, source_target_pairs={{0,4},{4,8},{8,12},{12,16},{16,20},{20,24},{24,28},{1,5},{5,9},{9,... | collective-permute-start | bytes 196616 | tf_op jit(solution)/shard_map/while/body/eval_jaxpr/ppermute | solution.py:12
  295.2 6.5 collective-permute-start
  303.0 13.1 %collective-permute-start = (bf16[64,512]{1,0:T(8,128)(2,1)S(1)}, bf16[64,512]{1,0:T(8,128)(2,1)S(1)}, u32[]{:S(2)}, u32[]{:S(2)}) collective-permute-start(bf16[64,512]{1,0:T(8,128)(2,1)S(1)} %get-tuple-element.520), channel_id=1, source_target_pairs={{0,4},{4,8},{8,12},{12,16},{16,20},{20,24},{24,28},{1,5},{5,9},{9,... | collective-permute-start | bytes 196616 | tf_op jit(solution)/shard_map/while/body/eval_jaxpr/ppermute | solution.py:12
  317.5 6.5 collective-permute-start
  325.3 13.1 %collective-permute-start = (bf16[64,512]{1,0:T(8,128)(2,1)S(1)}, bf16[64,512]{1,0:T(8,128)(2,1)S(1)}, u32[]{:S(2)}, u32[]{:S(2)}) collective-permute-start(bf16[64,512]{1,0:T(8,128)(2,1)S(1)} %get-tuple-element.520), channel_id=1, source_target_pairs={{0,4},{4,8},{8,12},{12,16},{16,20},{20,24},{24,28},{1,5},{5,9},{9,... | collective-permute-start | bytes 196616 | tf_op jit(solution)/shard_map/while/body/eval_jaxpr/ppermute | solution.py:12
  346.0 5.9 collective-permute-start.1
  353.3 6.7 collective-permute-start.1
  361.3 6.6 collective-permute-start.1
  369.3 8.5 %collective-permute-start.1 = (bf16[64,512]{1,0:T(8,128)(2,1)S(1)}, bf16[64,512]{1,0:T(8,128)(2,1)S(1)}, u32[]{:S(2)}, u32[]{:S(2)}) collective-permute-start(bf16[64,512]{1,0:T(8,128)(2,1)S(1)} %get-tuple-element.534), channel_id=1, source_target_pairs={{4,0},{8,4},{12,8},{16,12},{20,16},{24,20},{28,24},{5,1},{9,5},{13... | collective-permute-start | bytes 196616 | tf_op jit(solution)/shard_map/while/body/eval_jaxpr/ppermute | solution.py:12
  379.1 6.6 collective-permute-start.1
  387.0 6.6 collective-permute-start.1
  395.0 62.2 %collective-permute-start.1 = (bf16[64,512]{1,0:T(8,128)(2,1)S(1)}, bf16[64,512]{1,0:T(8,128)(2,1)S(1)}, u32[]{:S(2)}, u32[]{:S(2)}) collective-permute-start(bf16[64,512]{1,0:T(8,128)(2,1)S(1)} %get-tuple-element.534), channel_id=1, source_target_pairs={{4,0},{8,4},{12,8},{16,12},{20,16},{24,20},{28,24},{5,1},{9,5},{13... | collective-permute-start | bytes 196616 | tf_op jit(solution)/shard_map/while/body/eval_jaxpr/ppermute | solution.py:12
  458.4 6.9 copy-start.4
  467.2 6.6 collective-permute-start.1
  475.1 6.9 copy-start.4
  483.9 6.6 collective-permute-start.1
  491.8 6.9 copy-start.4
  500.6 6.6 collective-permute-start.1
  508.5 6.9 copy-start.4
  517.3 6.6 collective-permute-start.1
  525.1 6.9 copy-start.4
  534.0 6.6 collective-permute-start.1
  541.8 6.9 copy-start.4
  550.7 6.6 collective-permute-start.1
  558.5 6.9 copy-start.4
  567.4 6.6 collective-permute-start.1
  575.3 6.9 copy-start.4
  584.1 6.6 collective-permute-start.1
  592.0 6.9 copy-start.4
  600.8 6.6 collective-permute-start.1
  608.7 6.9 copy-start.4
  617.6 6.6 collective-permute-start.1
  625.4 6.9 copy-start.4
  634.2 6.6 collective-permute-start.1
  642.1 6.9 copy-start.4
  650.9 6.0 collective-permute-start.1
  663.5 1.9 copy-start.1
  663.6 155.8 %reduce-scatter.3.cloned.1.call-start = ((), (), s32[]{:S(2)}) async-start(), calls=%async_computation.4 | async-start | bytes 5242880 | tf_op jit(solution)/shard_map/reduce_scatter | solution.py:129
  671.2 68.6 %copy-start.2 = (bf16[1,4,128,512]{3,2,1,0:T(8,128)(2,1)S(1)}, bf16[1,4,128,512]{3,2,1,0:T(8,128)(2,1)}, u32[]{:S(2)}) copy-start(bf16[1,4,128,512]{3,2,1,0:T(8,128)(2,1)} %param.15) | copy-start | bytes 1572868
  671.2 148.2 %copy-start.3 = (bf16[1,4,128,512]{3,2,1,0:T(8,128)(2,1)S(1)}, bf16[1,4,128,512]{3,2,1,0:T(8,128)(2,1)}, u32[]{:S(2)}) copy-start(bf16[1,4,128,512]{3,2,1,0:T(8,128)(2,1)} %param.14) | copy-start | bytes 1572868
Sparse Core Ops, SparseCore 0:
  9.6 45.4 all-gather.2
  56.6 44.6 all-gather.4
  663.7 76.0 reduce-scatter.4
  742.0 77.2 reduce-scatter.2
where the time goes:
time: 839 us; the launch traced here: 828 us
  waiting for transfers between devices  308 us (37%)
  matrix products  171 us (20%)
  starting transfers between devices  121 us (14%)
  local copies, waits for them, and re-layouts  108 us (13%)
  other arithmetic  77.8 us (9%)
  loops' own time  27.8 us (3%)
  between operations  13.8 us (2%)
    ppermute x38, starting transfers between devices, shifted(): lax.ppermute(value, axis, [(source, source + steps) for source in range(i...  121 us
    reduce_scatter x1, waiting for transfers between devices, per_device(): lax.psum_scatter(grad_in, 'dp', scatter_dimension=1, tiled=True)  77.2 us
    dynamic_slice x76, local copies, waits for them, and re-layouts, put(): old = lax.dynamic_index_in_dim(store, index, axis_pos, keepdims=False)  74.4 us
    dot_general x48, matrix products, forward_section(): jnp.dot(hidden, second[layer], preferred_element_type=jnp.float32)  68.7 us
    reduce_scatter x1, waiting for transfers between devices, per_device(): lax.psum_scatter(grad_out, 'dp', scatter_dimension=1, tiled=True)  68.6 us
    ppermute x38, waiting for transfers between devices, shifted(): lax.ppermute(value, axis, [(source, source + steps) for source in range(i...  68.3 us
    dot_general x48, matrix products, backward_section(): pre = jnp.dot(value, first[layer], preferred_element_type=jnp.float32)  50.1 us
    dynamic_update_slice x57, other arithmetic, put(): lax.dynamic_update_index_in_dim(store, jnp.where(valid, fresh, old), inde...  47.2 us
  transfers between devices with their start and end apart: 42, of which 21 were waited for; matrix products, arithmetic and copies ran while one was open for 16% of the time, Pallas kernels for 0%

commit v1 on v0

v1 whole, which is shorter than its diff:
```python
import functools
import math

import jax
import jax.numpy as jnp
from jax import lax
from jax.experimental import pallas as pl
from jax.experimental.pallas import tpu as pltpu
from jax.sharding import PartitionSpec as P

MESH = pl.DeviceIdType.MESH
GROUP = 2
ROWS = 128


def kernel(
    n_s, n_d, group, tile, rate,
    img, cot, w_in, w_out, new_in, new_out,
    xs, hs, ds, dps, dys, ysend, dxsend, full_in, full_out, acc, gsend, grecv,
    f_tx, f_rx, b_tx, b_rx, w_tx, w_rx, g_tx, g_rx, e_tx, e_rx,
):
    s, d = lax.axis_index("section"), lax.axis_index("dp")
    layers, wr, width = w_in.shape[1:]
    per = layers // group
    part = img.shape[0]
    rows = group * part
    micro = rows // tile
    micro_part = part // tile
    reps = n_d // group
    stages = n_s * group

    b = lax.rem(d, group)
    even = lax.rem(s, 2) == 0
    half = jnp.where(even, b, group - 1 - b)
    stage = s * group + half
    step_dir = jnp.where(even, 1, -1)
    last = half == group - 1
    head = half == 0
    nxt_s = jnp.where(last, jnp.minimum(s + 1, n_s - 1), s)
    nxt_d = jnp.where(last, d, d + step_dir)
    prv_s = jnp.where(head, jnp.maximum(s - 1, 0), s)
    prv_d = jnp.where(head, d, d - step_dir)
    b_end = 0 if n_s % 2 == 0 else group - 1
    NT = (((1,), (1,)), ((), ()))
    TN = (((0,), (0,)), ((), ()))

    barrier = pltpu.get_barrier_semaphore()
    for o in range(1, n_d):
        pl.semaphore_signal(barrier, inc=1, device_id=(s, lax.rem(d + o, n_d)), device_id_type=MESH)

    @pl.when(s > 0)
    def _():
        pl.semaphore_signal(barrier, inc=1, device_id=(s - 1, d), device_id_type=MESH)

    @pl.when(s < n_s - 1)
    def _():
        pl.semaphore_signal(barrier, inc=1, device_id=(s + 1, d), device_id_type=MESH)

    pl.semaphore_wait(
        barrier, n_d - 1 + jnp.where(s > 0, 1, 0) + jnp.where(s < n_s - 1, 1, 0)
    )

    mats = ((w_in, full_in), (w_out, full_out))

    def half_of(dev):
        bb = lax.rem(dev, group)
        return jnp.where(even, bb, group - 1 - bb)

    def block(i, count):
        return pl.ds(pl.multiple_of(i * count, count), count)

    def weight_copy(mat, k, o, at):
        t = lax.rem(d + o, n_d)
        src, dst = mats[mat]
        return pltpu.make_async_remote_copy(
            src_ref=src.at[0, half_of(t) * per + k],
            dst_ref=dst.at[k, block(at, wr)],
            send_sem=w_tx.at[mat, k, o - 1],
            recv_sem=w_rx.at[mat, k, o - 1],
            device_id=(s, t),
            device_id_type=MESH,
        )

    def extra_copy(which, target_b, at):
        src, dst = ((img, xs.at[0]), (cot, dys.at[per - 1]))[which]
        return pltpu.make_async_remote_copy(
            src_ref=src,
            dst_ref=dst.at[block(at, part)],
            send_sem=e_tx.at[which],
            recv_sem=e_rx.at[which, at],
            device_id=(s, d - b + target_b),
            device_id_type=MESH,
        )

    for k in range(per):
        for mat in range(2):
            for o in range(1, n_d):
                weight_copy(mat, k, o, d).start()
    if group > 1:
        @pl.when((s == 0) & (b != 0))
        def _():
            extra_copy(0, 0, b).start()

        @pl.when((s == n_s - 1) & (b != b_end))
        def _():
            extra_copy(1, b_end, b).start()

    for src, dst in mats:
        for k in range(per):
            dst[k, block(d, wr), :] = src[0, half * per + k]

    @pl.when(stage == 0)
    def _():
        xs[0, pl.ds(0, part), :] = img[...]

    @pl.when(stage == stages - 1)
    def _():
        dys[per - 1, pl.ds(b_end * part, part), :] = cot[...]

    def forward_copy(m):
        return pltpu.make_async_remote_copy(
            src_ref=ysend.at[block(m, tile)],
            dst_ref=xs.at[0, block(m, tile)],
            send_sem=f_tx.at[m],
            recv_sem=f_rx.at[m],
            device_id=(nxt_s, nxt_d),
            device_id_type=MESH,
        )

    def backward_copy(m):
        return pltpu.make_async_remote_copy(
            src_ref=dxsend.at[block(m, tile)],
            dst_ref=dys.at[per - 1, block(m, tile)],
            send_sem=b_tx.at[m],
            recv_sem=b_rx.at[m],
            device_id=(prv_s, prv_d),
            device_id_type=MESH,
        )

    def weights_here(mat, k):
        for o in range(1, n_d):
            weight_copy(mat, k, o, lax.rem(d + n_d - o, n_d)).wait_recv()

    def forward(m, carry):
        at = block(m, tile)

        @pl.when(stage > 0)
        def _():
            forward_copy(m).wait_recv()

        for bb in range(1, group):
            @pl.when((stage == 0) & (m == bb * micro_part))
            def _():
                extra_copy(0, 0, bb).wait_recv()

        for k in range(per):
            @pl.when(m == 0)
            def _():
                weights_here(0, k)

            x = xs[k, at, :]
            pre = jnp.dot(x, full_in[k], preferred_element_type=jnp.float32)
            sig = jax.nn.sigmoid(pre)
            h = (pre * sig).astype(jnp.bfloat16)
            hs[k, at, :] = h
            ds[k, at, :] = sig * (1.0 + pre * (1.0 - sig))

            @pl.when(m == 0)
            def _():
                weights_here(1, k)

            y = (
                x.astype(jnp.float32)
                + jnp.dot(h, full_out[k], preferred_element_type=jnp.float32)
            ).astype(jnp.bfloat16)
            if k + 1 < per:
                xs[k + 1, at, :] = y
            else:
                ysend[at, :] = y

        @pl.when(stage < stages - 1)
        def _():
            forward_copy(m).start()

        return carry

    lax.fori_loop(0, micro, forward, 0)

    def backward(m, carry):
        at = block(m, tile)

        @pl.when(stage < stages - 1)
        def _():
            backward_copy(m).wait_recv()

        for bb in range(group):
            if bb != b_end:
                @pl.when((stage == stages - 1) & (m == bb * micro_part))
                def _():
                    extra_copy(1, b_end, bb).wait_recv()

        for k in reversed(range(per)):
            dy = dys[k, at, :]
            dh = lax.dot_general(dy, full_out[k], NT, preferred_element_type=jnp.float32)
            dp = (dh * ds[k, at, :]).astype(jnp.bfloat16)
            dps[k, at, :] = dp
            dx = (
                dy.astype(jnp.float32)
                + lax.dot_general(dp, full_in[k], NT, preferred_element_type=jnp.float32)
            ).astype(jnp.bfloat16)
            if k > 0:
                dys[k - 1, at, :] = dx
            else:
                dxsend[at, :] = dx

        @pl.when(stage > 0)
        def _():
            backward_copy(m).start()

        return carry

    lax.fori_loop(0, micro, backward, 0)

    rep = d // group

    def grad_copy(mat, k, o):
        t = lax.rem(d + o, n_d)
        layer = half * per + k
        return pltpu.make_async_remote_copy(
            src_ref=gsend.at[mat, k, block(t, wr)],
            dst_ref=grecv.at[mat, rep, layer],
            send_sem=g_tx.at[mat, k, o - 1],
            recv_sem=g_rx.at[mat, rep, layer],
            device_id=(s, t),
            device_id_type=MESH,
        )

    chunk = part
    for k in reversed(range(per)):
        for mat in (1, 0):
            left, right = ((xs, dps), (hs, dys))[mat]
            for c in range(rows // chunk):
                term = lax.dot_general(
                    left[k, pl.ds(c * chunk, chunk), :],
                    right[k, pl.ds(c * chunk, chunk), :],
                    TN, preferred_element_type=jnp.float32,
                )
                if c + 1 < rows // chunk:
                    acc[...] = term if c == 0 else acc[...] + term
                else:
                    total = term if c == 0 else acc[...] + term
                    gsend[mat, k] = total.astype(jnp.bfloat16)
            for o in range(1, n_d):
                grad_copy(mat, k, o).start()
            grecv[mat, rep, half * per + k] = gsend[mat, k, block(d, wr), :]

    for layer in reversed(range(layers)):
        owner_half = layer // per
        for mat in (1, 0):
            for r in range(reps):
                host = r * group + jnp.where(even, owner_half, group - 1 - owner_half)

                @pl.when(host != d)
                def _():
                    pltpu.make_async_remote_copy(
                        src_ref=gsend.at[mat, 0, pl.ds(0, wr)],
                        dst_ref=grecv.at[mat, r, layer],
                        send_sem=g_tx.at[mat, 0, 0],
                        recv_sem=g_rx.at[mat, r, layer],
                        device_id=(s, host),
                        device_id_type=MESH,
                    ).wait_recv()

            total = grecv[mat, 0, layer].astype(jnp.float32)
            for r in range(1, reps):
                total += grecv[mat, r, layer].astype(jnp.float32)
            w, out = ((w_in, new_in), (w_out, new_out))[mat]
            out[0, layer] = w[0, layer].astype(jnp.float32) - rate * total

    for mat in range(2):
        for k in range(per):
            for o in range(1, n_d):
                weight_copy(mat, k, o, d).wait_send()
                grad_copy(mat, k, o).wait_send()
    if group > 1:
        @pl.when((s == 0) & (b != 0))
        def _():
            extra_copy(0, 0, b).wait_send()

        @pl.when((s == n_s - 1) & (b != b_end))
        def _():
            extra_copy(1, b_end, b).wait_send()

    def drain(m, carry):
        @pl.when(stage < stages - 1)
        def _():
            forward_copy(m).wait_send()

        @pl.when(stage > 0)
        def _():
            backward_copy(m).wait_send()

        return carry

    lax.fori_loop(0, micro, drain, 0)


def solution(mesh):
    n_s, n_d = mesh.shape["section"], mesh.shape["dp"]

    def per_device(images, cotangent, w_in, w_out):
        micro, pixels, width = images.shape
        layers, wr = w_in.shape[1:3]
        part = micro * pixels
        group, tile = GROUP, ROWS
        rows, per, reps = group * part, layers // group, n_d // group
        steps = rows // tile
        bf, f32 = jnp.bfloat16, jnp.float32
        rate = 0.1 / math.sqrt(part * n_d)
        dma = pltpu.SemaphoreType.DMA
        vmem = pl.BlockSpec(memory_space=pltpu.VMEM)
        return pl.pallas_call(
            functools.partial(kernel, n_s, n_d, group, tile, rate),
            out_shape=(
                jax.ShapeDtypeStruct(w_in.shape, f32),
                jax.ShapeDtypeStruct(w_out.shape, f32),
            ),
            in_specs=[vmem] * 4,
            out_specs=(vmem, vmem),
            scratch_shapes=[
                pltpu.VMEM((per, rows, width), bf),
                pltpu.VMEM((per, rows, width), bf),
                pltpu.VMEM((per, rows, width), f32),
                pltpu.VMEM((per, rows, width), bf),
                pltpu.VMEM((per, rows, width), bf),
                pltpu.VMEM((rows, width), bf),
                pltpu.VMEM((rows, width), bf),
                pltpu.VMEM((per, width, width), bf),
                pltpu.VMEM((per, width, width), bf),
                pltpu.VMEM((width, width), f32),
                pltpu.VMEM((2, per, width, width), bf),
                pltpu.VMEM((2, reps, layers, wr, width), bf),
                dma((steps,)), dma((steps,)), dma((steps,)), dma((steps,)),
                dma((2, per, n_d - 1)), dma((2, per, n_d - 1)),
                dma((2, per, n_d - 1)), dma((2, reps, layers)),
                dma((2,)), dma((2, group)),
            ],
            compiler_params=pltpu.CompilerParams(
                collective_id=0, has_side_effects=True, vmem_limit_bytes=56 * 1024 * 1024
            ),
            cost_estimate=pl.CostEstimate(
                flops=12 * part * layers * width * width, bytes_accessed=8 << 20, transcendentals=0
            ),
        )(images.reshape(part, width), cotangent.reshape(part, width), w_in, w_out)

    in_specs = (
        P(None, "dp", None),
        P(None, "dp", None),
        P("section", None, "dp", None),
        P("section", None, "dp", None),
    )
    out_specs = (P("section", None, "dp", None), P("section", None, "dp", None))
    return jax.shard_map(
        per_device, mesh=mesh, in_specs=in_specs, out_specs=out_specs, check_vma=False
    )
```

time: 839 us -> 276 us (0.33); the launches traced: 828 us -> 274 us
  waiting for transfers between devices: 308 us -> 0 us
  Pallas kernels: 0 us -> 270 us
  matrix products: 171 us -> 0 us
  starting transfers between devices: 121 us -> 0 us
  local copies, waits for them, and re-layouts: 108 us -> 3.32 us
  other arithmetic: 77.8 us -> 0 us
  loops' own time: 27.8 us -> 0 us
  between operations: 13.8 us -> 0.65 us
    pallas_call x0 -> x1, Pallas kernels: none -> 270 us  [per_device(): pl.pallas_call(functools.partial(kernel, n_s, n_d, group, tile, rate), ou...]
    dot_general x194 -> x0, matrix products: 171 us -> none  [the longest x48 68.7 us: forward_section(): jnp.dot(hidden, second[layer], preferred_element_type=jnp.float32)]
    reduce_scatter x2 -> x0, waiting for transfers between devices: 146 us -> none  [the longest x1 77.2 us: per_device(): lax.psum_scatter(grad_in, 'dp', scatter_dimension=1, tiled=True)]
    ppermute x38 -> x0, starting transfers between devices: 121 us -> none  [shifted(): lax.ppermute(value, axis, [(source, source + steps) for source in range(i...]
    dynamic_slice x114 -> x0, local copies, waits for them, and re-layouts: 97.5 us -> none  [the longest x76 74.4 us: put(): old = lax.dynamic_index_in_dim(store, index, axis_pos, keepdims=False)]
    all_gather x2 -> x0, waiting for transfers between devices: 92.6 us -> none  [the longest x1 46.4 us: per_device(): lax.all_gather(w_in, 'dp', axis=2, tiled=True)]
    ppermute x38 -> x0, waiting for transfers between devices: 68.3 us -> none  [shifted(): lax.ppermute(value, axis, [(source, source + steps) for source in range(i...]
    dynamic_update_slice x57 -> x0, other arithmetic: 47.2 us -> none  [put(): lax.dynamic_update_index_in_dim(store, jnp.where(valid, fresh, old), inde...]
  transfers between devices with their start and end apart: 42 -> 0, of which waited for: 21 -> 0; matrix products, arithmetic and copies ran while one was open for 16% -> 0% of each run, Pallas kernels for 0% -> 0%
where the time goes in v1:
time: 276 us; the launch traced here: 274 us
  Pallas kernels  270 us (98%)
  local copies, waits for them, and re-layouts  3.32 us (1%)
    pallas_call x1, Pallas kernels, per_device(): pl.pallas_call(functools.partial(kernel, n_s, n_d, group, tile, rate), ou...  270 us

profile of v1, /device:TPU:8, one launch (start us, length us, event | category | flops | bytes accessed | tf_op | source)
XLA Modules:
  0.0 274.4 jit_solution(5888258619606426003)
XLA Ops:
  0.6 270.4 %shard_map.59 = (f32[1,4,128,512]{3,2,1,0:T(8,128)}, f32[1,4,128,512]{3,2,1,0:T(8,128)}) custom-call(bf16[768,512]{1,0:T(8,128)(2,1)} %bitcast.2, bf16[768,512]{1,0:T(8,128)(2,1)} %bitcast.3, bf16[1,4,128,512]{3,2,1,0:T(8,128)(2,1)} %w_in.1, bf16[1,4,128,512]{3,2,1,0:T(8,128)(2,1)} %w_out.1), custom_call_target="tpu_custom_call" | custom-call | flops 9663676416 | bytes 8388608 | tf_op jit(solution)/shard_map/pallas_call | solution.py:322
  271.1 0.0 copy-start
  271.1 2.4 copy.8
  273.4 0.0 copy-done
  273.4 1.0 copy.9
Async XLA Ops:
  271.1 2.4 copy-start

commit v2 on v1

v2 whole, which is shorter than its diff:
```python
import functools
import math

import jax
import jax.numpy as jnp
from jax import lax
from jax.experimental import pallas as pl
from jax.experimental.pallas import tpu as pltpu
from jax.sharding import PartitionSpec as P

MESH = pl.DeviceIdType.MESH
GROUP = 2
ROWS = 64


def kernel(
    n_s, n_d, group, tile, rate,
    img, cot, w_in, w_out, new_in, new_out,
    left, right, ds, ysend, dxsend, full, acc, gsend, gpeer, gtotal, grecv,
    f_tx, f_rx, b_tx, b_rx, w_tx, w_rx, p_tx, g_tx, g_rx, x_tx, x_rx, e_tx, e_rx,
):
    s, d = lax.axis_index("section"), lax.axis_index("dp")
    layers, wr, width = w_in.shape[1:]
    per = 2 * layers // group
    part = img.shape[0]
    share = group // 2
    rows = share * part
    micro = rows // tile
    micro_part = part // tile
    reps = n_d // group
    columns = n_s // 2
    stages = columns * group

    col, core = s // 2, lax.rem(s, 2)
    mate = 2 * col + 1 - core
    b = lax.rem(d, group)
    base = d - b
    rep = d // group
    even = lax.rem(col, 2) == 0
    half = jnp.where(even, b, group - 1 - b)
    stage = col * group + half
    step_dir = jnp.where(even, 1, -1)
    last = half == group - 1
    head = half == 0
    nxt_s = jnp.where(last, jnp.minimum(s + 2, n_s - 2 + core), s)
    nxt_d = jnp.where(last, d, d + step_dir)
    prv_s = jnp.where(head, jnp.maximum(s - 2, core), s)
    prv_d = jnp.where(head, d, d - step_dir)
    b_end = 0 if columns % 2 == 0 else group - 1
    NT = (((1,), (1,)), ((), ()))
    TN = (((0,), (0,)), ((), ()))

    barrier = pltpu.get_barrier_semaphore()
    pl.semaphore_signal(barrier, inc=1, device_id=(mate, d), device_id_type=MESH)
    for o in range(1, n_d):
        for cc in range(2):
            pl.semaphore_signal(
                barrier, inc=1, device_id=(2 * col + cc, lax.rem(d + o, n_d)), device_id_type=MESH
            )

    @pl.when(col > 0)
    def _():
        pl.semaphore_signal(barrier, inc=1, device_id=(s - 2, d), device_id_type=MESH)

    @pl.when(col < columns - 1)
    def _():
        pl.semaphore_signal(barrier, inc=1, device_id=(s + 2, d), device_id_type=MESH)

    pl.semaphore_wait(
        barrier,
        2 * n_d - 1 + jnp.where(col > 0, 1, 0) + jnp.where(col < columns - 1, 1, 0),
    )

    def host(r, h):
        return r * group + jnp.where(even, h, group - 1 - h)

    def block(i, count):
        return pl.ds(pl.multiple_of(i * count, count), count)

    def weight_copy(mat, layer, r):
        t = host(r, (core * layers + layer) // per)
        return pltpu.make_async_remote_copy(
            src_ref=(w_in, w_out)[mat].at[0, layer],
            dst_ref=full.at[mat, layer % per, block(d, wr)],
            send_sem=w_tx.at[mat, layer, r],
            recv_sem=w_rx.at[mat, layer % per, d],
            device_id=(jnp.where(t == d, mate, 2 * col + mat), t),
            device_id_type=MESH,
        )

    def pass_copy(mat, k, zz, slot):
        ref = full.at[mat, k, block(zz, wr)]
        return pltpu.make_async_remote_copy(
            src_ref=ref,
            dst_ref=ref,
            send_sem=p_tx.at[k, slot],
            recv_sem=w_rx.at[mat, k, zz],
            device_id=(mate, d),
            device_id_type=MESH,
        )

    def extra_copy(which, target_b, at):
        src, dst = ((img, left.at[0, 0]), (cot, right.at[1, per - 1]))[which]
        return pltpu.make_async_remote_copy(
            src_ref=src,
            dst_ref=dst.at[block(at, part)],
            send_sem=e_tx.at[which],
            recv_sem=e_rx.at[which, at],
            device_id=(s, base + target_b),
            device_id_type=MESH,
        )

    feeds = (b // share) == core
    feed_in = (col == 0) & (b != 0) & feeds
    feed_out = (col == columns - 1) & (b != b_end) & feeds
    slot_of = lax.rem(b, share)

    @pl.when(feed_in)
    def _():
        extra_copy(0, 0, slot_of).start()

    for layer in range(layers):
        for mat in range(2):
            for r in range(reps):
                weight_copy(mat, layer, r).start()

    @pl.when(feed_out)
    def _():
        extra_copy(1, b_end, slot_of).start()

    for k in range(per):
        e = half * per + k

        @pl.when(e // layers == core)
        def _():
            full[0, k, block(d, wr), :] = w_in[0, lax.rem(e, layers)]
            full[1, k, block(d, wr), :] = w_out[0, lax.rem(e, layers)]

    @pl.when((stage == 0) & (core == 0))
    def _():
        left[0, 0, pl.ds(0, part), :] = img[...]

    @pl.when((stage == stages - 1) & (core == b_end // share))
    def _():
        right[1, per - 1, pl.ds((b_end % share) * part, part), :] = cot[...]

    def forward_copy(m):
        return pltpu.make_async_remote_copy(
            src_ref=ysend.at[block(m, tile)],
            dst_ref=left.at[0, 0, block(m, tile)],
            send_sem=f_tx.at[m],
            recv_sem=f_rx.at[m],
            device_id=(nxt_s, nxt_d),
            device_id_type=MESH,
        )

    def backward_copy(m):
        return pltpu.make_async_remote_copy(
            src_ref=dxsend.at[block(m, tile)],
            dst_ref=right.at[1, per - 1, block(m, tile)],
            send_sem=b_tx.at[m],
            recv_sem=b_rx.at[m],
            device_id=(prv_s, prv_d),
            device_id_type=MESH,
        )

    def weights_here(k):
        for o in range(1, n_d):
            zz = lax.rem(d + o, n_d)
            arrived = pass_copy(core, k, zz, o - 1)
            arrived.wait_recv()
            arrived.start()

        @pl.when((half * per + k) // layers != core)
        def _():
            pass_copy(0, k, d, 0).wait_recv()
            pass_copy(1, k, d, 0).wait_recv()

        for o in range(1, n_d):
            pass_copy(1 - core, k, lax.rem(d + o, n_d), o - 1).wait_recv()

    @pl.when(stage > 0)
    def _():
        for k in range(per):
            weights_here(k)

    def forward(m, carry):
        at = block(m, tile)

        @pl.when(stage > 0)
        def _():
            forward_copy(m).wait_recv()

        for i in range(share):
            for cc in range(2):
                if i + cc > 0:
                    @pl.when((stage == 0) & (core == cc) & (m == i * micro_part))
                    def _():
                        extra_copy(0, 0, i).wait_recv()

        for k in range(per):
            @pl.when((stage == 0) & (m == 0))
            def _():
                weights_here(k)

            x = left[0, k, at, :]
            pre = jnp.dot(x, full[0, k], preferred_element_type=jnp.float32)
            sig = jax.nn.sigmoid(pre)
            h = (pre * sig).astype(jnp.bfloat16)
            left[1, k, at, :] = h
            ds[k, at, :] = sig * (1.0 + pre * (1.0 - sig))
            y = (
                x.astype(jnp.float32)
                + jnp.dot(h, full[1, k], preferred_element_type=jnp.float32)
            ).astype(jnp.bfloat16)
            if k + 1 < per:
                left[0, k + 1, at, :] = y
            else:
                ysend[at, :] = y

        @pl.when(stage < stages - 1)
        def _():
            forward_copy(m).start()

        return carry

    lax.fori_loop(0, micro, forward, 0)

    def backward(m, carry):
        at = block(m, tile)

        @pl.when(stage < stages - 1)
        def _():
            backward_copy(m).wait_recv()

        for i in range(share):
            for cc in range(2):
                if cc * share + i != b_end:
                    @pl.when((stage == stages - 1) & (core == cc) & (m == i * micro_part))
                    def _():
                        extra_copy(1, b_end, i).wait_recv()

        for k in reversed(range(per)):
            dy = right[1, k, at, :]
            dh = lax.dot_general(dy, full[1, k], NT, preferred_element_type=jnp.float32)
            dp = (dh * ds[k, at, :]).astype(jnp.bfloat16)
            right[0, k, at, :] = dp
            dx = (
                dy.astype(jnp.float32)
                + lax.dot_general(dp, full[0, k], NT, preferred_element_type=jnp.float32)
            ).astype(jnp.bfloat16)
            if k > 0:
                right[1, k - 1, at, :] = dx
            else:
                dxsend[at, :] = dx

        @pl.when(stage > 0)
        def _():
            backward_copy(m).start()

        return carry

    lax.fori_loop(0, micro, backward, 0)

    def swap_copy(k):
        return pltpu.make_async_remote_copy(
            src_ref=gsend.at[k],
            dst_ref=gpeer.at[k],
            send_sem=x_tx.at[k],
            recv_sem=x_rx.at[k],
            device_id=(mate, d),
            device_id_type=MESH,
        )

    def grad_copy(k, t, slot):
        e = half * per + k
        return pltpu.make_async_remote_copy(
            src_ref=gtotal.at[k, block(t, wr)],
            dst_ref=grecv.at[core, rep, lax.rem(e, layers)],
            send_sem=g_tx.at[k, slot],
            recv_sem=g_rx.at[core, rep, lax.rem(e, layers)],
            device_id=(2 * col + e // layers, t),
            device_id_type=MESH,
        )

    def product(mat, k):
        for c in range(share):
            at = pl.ds(c * part, part)
            term = lax.dot_general(
                left[mat, k, at, :], right[mat, k, at, :], TN, preferred_element_type=jnp.float32
            )
            acc[...] = term if c == 0 else acc[...] + term

    for k in reversed(range(per)):
        e = half * per + k
        product(1 - core, k)
        gsend[k] = acc[...].astype(jnp.bfloat16)
        swap_copy(k).start()
        product(core, k)
        swap_copy(k).wait_recv()
        gtotal[k] = (acc[...] + gpeer[k].astype(jnp.float32)).astype(jnp.bfloat16)
        for o in range(1, n_d):
            grad_copy(k, lax.rem(d + o, n_d), o).start()

        @pl.when(e // layers != core)
        def _():
            grad_copy(k, d, 0).start()

        @pl.when(e // layers == core)
        def _():
            grecv[core, rep, lax.rem(e, layers)] = gtotal[k, block(d, wr), :]

    for layer in reversed(range(layers)):
        for mat in (1, 0):
            for r in range(reps):
                t = host(r, (core * layers + layer) // per)

                @pl.when((t != d) | (core != mat))
                def _():
                    pltpu.make_async_remote_copy(
                        src_ref=gtotal.at[0, pl.ds(0, wr)],
                        dst_ref=grecv.at[mat, r, layer],
                        send_sem=g_tx.at[0, 0],
                        recv_sem=g_rx.at[mat, r, layer],
                        device_id=(mate, d),
                        device_id_type=MESH,
                    ).wait_recv()

            total = grecv[mat, 0, layer].astype(jnp.float32)
            for r in range(1, reps):
                total += grecv[mat, r, layer].astype(jnp.float32)
            w, out = ((w_in, new_in), (w_out, new_out))[mat]
            out[0, layer] = w[0, layer].astype(jnp.float32) - rate * total

    for layer in range(layers):
        for mat in range(2):
            for r in range(reps):
                weight_copy(mat, layer, r).wait_send()
    for k in range(per):
        e = half * per + k
        swap_copy(k).wait_send()
        for o in range(1, n_d):
            pass_copy(core, k, lax.rem(d + o, n_d), o - 1).wait_send()
            grad_copy(k, lax.rem(d + o, n_d), o).wait_send()

        @pl.when(e // layers != core)
        def _():
            grad_copy(k, d, 0).wait_send()

    @pl.when(feed_in)
    def _():
        extra_copy(0, 0, slot_of).wait_send()

    @pl.when(feed_out)
    def _():
        extra_copy(1, b_end, slot_of).wait_send()

    def drain(m, carry):
        @pl.when(stage < stages - 1)
        def _():
            forward_copy(m).wait_send()

        @pl.when(stage > 0)
        def _():
            backward_copy(m).wait_send()

        return carry

    lax.fori_loop(0, micro, drain, 0)


def solution(mesh):
    n_s, n_d = mesh.shape["section"], mesh.shape["dp"]

    def per_device(images, cotangent, w_in, w_out):
        micro, pixels, width = images.shape
        layers, wr = w_in.shape[1:3]
        part = micro * pixels
        group, tile = GROUP, ROWS
        rows, per, reps = group // 2 * part, 2 * layers // group, n_d // group
        steps = rows // tile
        bf, f32 = jnp.bfloat16, jnp.float32
        rate = 0.1 / math.sqrt(part * n_d)
        dma = pltpu.SemaphoreType.DMA
        vmem = pl.BlockSpec(memory_space=pltpu.VMEM)
        return pl.pallas_call(
            functools.partial(kernel, n_s, n_d, group, tile, rate),
            out_shape=(
                jax.ShapeDtypeStruct(w_in.shape, f32),
                jax.ShapeDtypeStruct(w_out.shape, f32),
            ),
            in_specs=[vmem] * 4,
            out_specs=(vmem, vmem),
            scratch_shapes=[
                pltpu.VMEM((2, per, rows, width), bf),
                pltpu.VMEM((2, per, rows, width), bf),
                pltpu.VMEM((per, rows, width), f32),
                pltpu.VMEM((rows, width), bf),
                pltpu.VMEM((rows, width), bf),
                pltpu.VMEM((2, per, width, width), bf),
                pltpu.VMEM((width, width), f32),
                pltpu.VMEM((per, width, width), bf),
                pltpu.VMEM((per, width, width), bf),
                pltpu.VMEM((per, width, width), bf),
                pltpu.VMEM((2, reps, layers, wr, width), bf),
                dma((steps,)), dma((steps,)), dma((steps,)), dma((steps,)),
                dma((2, layers, reps)), dma((2, per, n_d)), dma((per, n_d - 1)),
                dma((per, n_d)), dma((2, reps, layers)),
                dma((per,)), dma((per,)),
                dma((2,)), dma((2, group // 2)),
            ],
            compiler_params=pltpu.CompilerParams(
                collective_id=0, has_side_effects=True, vmem_limit_bytes=56 * 1024 * 1024
            ),
            cost_estimate=pl.CostEstimate(
                flops=12 * part * layers * width * width, bytes_accessed=8 << 20, transcendentals=0
            ),
        )(images.reshape(part, width), cotangent.reshape(part, width), w_in, w_out)

    in_specs = (
        P(None, "dp", None),
        P(None, "dp", None),
        P("section", None, "dp", None),
        P("section", None, "dp", None),
    )
    out_specs = (P("section", None, "dp", None), P("section", None, "dp", None))
    return jax.shard_map(
        per_device, mesh=mesh, in_specs=in_specs, out_specs=out_specs, check_vma=False
    )
```

time: 276 us -> 216 us (0.78)
  Pallas kernels: 270 us -> 212 us
    pallas_call x1, Pallas kernels: 270 us -> 212 us  [per_device(): pl.pallas_call(functools.partial(kernel, n_s, n_d, group, tile, rate), ou...]
where the time goes in v2:
time: 216 us
  Pallas kernels  212 us (98%)
  local copies, waits for them, and re-layouts  3.32 us (2%)
    pallas_call x1, Pallas kernels, per_device(): pl.pallas_call(functools.partial(kernel, n_s, n_d, group, tile, rate), ou...  212 us

profile of v2, /device:TPU:8, one launch (start us, length us, event | category | flops | bytes accessed | tf_op | source)
XLA Modules:
  0.0 215.9 jit_solution(18171059182035052112)
XLA Ops:
  0.6 211.9 %shard_map.59 = (f32[1,4,128,512]{3,2,1,0:T(8,128)}, f32[1,4,128,512]{3,2,1,0:T(8,128)}) custom-call(bf16[768,512]{1,0:T(8,128)(2,1)} %bitcast.2, bf16[768,512]{1,0:T(8,128)(2,1)} %bitcast.3, bf16[1,4,128,512]{3,2,1,0:T(8,128)(2,1)} %w_in.1, bf16[1,4,128,512]{3,2,1,0:T(8,128)(2,1)} %w_out.1), custom_call_target="tpu_custom_call" | custom-call | flops 9663676416 | bytes 8388608 | tf_op jit(solution)/shard_map/pallas_call | solution.py:386
  212.5 0.0 copy-start
  212.6 2.4 %copy.8 = f32[1,4,128,512]{3,2,1,0:T(8,128)} copy(f32[1,4,128,512]{3,2,1,0:T(8,128)} %get-tuple-element.4) | data formatting | bytes 2097152
  214.9 0.0 copy-done
  214.9 1.0 copy.9
Async XLA Ops:
  212.5 2.4 %copy-start = (f32[1,4,128,512]{3,2,1,0:T(8,128)S(1)}, f32[1,4,128,512]{3,2,1,0:T(8,128)}, u32[]{:S(2)}) copy-start(f32[1,4,128,512]{3,2,1,0:T(8,128)} %get-tuple-element.5) | copy-start | bytes 3145732

commit v3 on v2

--- a/solution.py
+++ b/solution.py
@@ -16,7 +16,7 @@
 def kernel(
     n_s, n_d, group, tile, rate,
     img, cot, w_in, w_out, new_in, new_out,
-    left, right, ds, ysend, dxsend, full, acc, gsend, gpeer, gtotal, grecv,
+    left, right, ds, ysend, dxsend, full, full_t, acc, gsend, gpeer, gtotal, grecv,
     f_tx, f_rx, b_tx, b_rx, w_tx, w_rx, p_tx, g_tx, g_rx, x_tx, x_rx, e_tx, e_rx,
 ):
     s, d = lax.axis_index("section"), lax.axis_index("dp")
@@ -47,7 +47,6 @@
     prv_s = jnp.where(head, jnp.maximum(s - 2, core), s)
     prv_d = jnp.where(head, d, d - step_dir)
     b_end = 0 if columns % 2 == 0 else group - 1
-    NT = (((1,), (1,)), ((), ()))
     TN = (((0,), (0,)), ((), ()))
 
     barrier = pltpu.get_barrier_semaphore()
@@ -224,7 +223,20 @@
 
         return carry
 
+    def transpose_weights():
+        for mat in range(2):
+            for k in range(per):
+                full_t[mat, k] = full[mat, k].T
+
+    @pl.when(stage >= stages // 2)
+    def _():
+        transpose_weights()
+
     lax.fori_loop(0, micro, forward, 0)
+
+    @pl.when(stage < stages // 2)
+    def _():
+        transpose_weights()
 
     def backward(m, carry):
         at = block(m, tile)
@@ -242,12 +254,12 @@
 
         for k in reversed(range(per)):
             dy = right[1, k, at, :]
-            dh = lax.dot_general(dy, full[1, k], NT, preferred_element_type=jnp.float32)
+            dh = jnp.dot(dy, full_t[1, k], preferred_element_type=jnp.float32)
             dp = (dh * ds[k, at, :]).astype(jnp.bfloat16)
             right[0, k, at, :] = dp
             dx = (
                 dy.astype(jnp.float32)
-                + lax.dot_general(dp, full[0, k], NT, preferred_element_type=jnp.float32)
+                + jnp.dot(dp, full_t[0, k], preferred_element_type=jnp.float32)
             ).astype(jnp.bfloat16)
             if k > 0:
                 right[1, k - 1, at, :] = dx
@@ -398,6 +410,7 @@
                 pltpu.VMEM((rows, width), bf),
                 pltpu.VMEM((rows, width), bf),
                 pltpu.VMEM((2, per, width, width), bf),
+                pltpu.VMEM((2, per, width, width), bf),
                 pltpu.VMEM((width, width), f32),
                 pltpu.VMEM((per, width, width), bf),
                 pltpu.VMEM((per, width, width), bf),

time: 216 us -> 211 us (0.977)
  Pallas kernels: 212 us -> 207 us
    pallas_call x1, Pallas kernels: 212 us -> 207 us  [per_device(): pl.pallas_call(functools.partial(kernel, n_s, n_d, group, tile, rate), ou...]
where the time goes in v3:
time: 211 us
  Pallas kernels  207 us (98%)
  local copies, waits for them, and re-layouts  3.32 us (2%)
    pallas_call x1, Pallas kernels, per_device(): pl.pallas_call(functools.partial(kernel, n_s, n_d, group, tile, rate), ou...  207 us

profile of v3, /device:TPU:8, one launch (start us, length us, event | category | flops | bytes accessed | tf_op | source)
XLA Modules:
  0.0 210.7 jit_solution(5557085552352693584)
XLA Ops:
  0.6 206.7 %shard_map.59 = (f32[1,4,128,512]{3,2,1,0:T(8,128)}, f32[1,4,128,512]{3,2,1,0:T(8,128)}) custom-call(bf16[768,512]{1,0:T(8,128)(2,1)} %bitcast.2, bf16[768,512]{1,0:T(8,128)(2,1)} %bitcast.3, bf16[1,4,128,512]{3,2,1,0:T(8,128)(2,1)} %w_in.1, bf16[1,4,128,512]{3,2,1,0:T(8,128)(2,1)} %w_out.1), custom_call_target="tpu_custom_call" | custom-call | flops 9663676416 | bytes 8388608 | tf_op jit(solution)/shard_map/pallas_call | solution.py:398
  207.3 0.0 copy-start
  207.4 2.4 %copy.8 = f32[1,4,128,512]{3,2,1,0:T(8,128)} copy(f32[1,4,128,512]{3,2,1,0:T(8,128)} %get-tuple-element.4) | data formatting | bytes 2097152
  209.7 0.0 copy-done
  209.7 1.0 copy.9
Async XLA Ops:
  207.3 2.4 %copy-start = (f32[1,4,128,512]{3,2,1,0:T(8,128)S(1)}, f32[1,4,128,512]{3,2,1,0:T(8,128)}, u32[]{:S(2)}) copy-start(f32[1,4,128,512]{3,2,1,0:T(8,128)} %get-tuple-element.5) | copy-start | bytes 3145732

commit v4 on v3

--- a/solution.py
+++ b/solution.py
@@ -120,8 +120,8 @@
 
     for layer in range(layers):
         for mat in range(2):
-            for r in range(reps):
-                weight_copy(mat, layer, r).start()
+            for r in range(1, reps + 1):
+                weight_copy(mat, layer, lax.rem(rep + r, reps)).start()
 
     @pl.when(feed_out)
     def _():
@@ -311,7 +311,7 @@
         product(core, k)
         swap_copy(k).wait_recv()
         gtotal[k] = (acc[...] + gpeer[k].astype(jnp.float32)).astype(jnp.bfloat16)
-        for o in range(1, n_d):
+        for o in sorted(range(1, n_d), key=lambda o: -min(o, n_d - o)):
             grad_copy(k, lax.rem(d + o, n_d), o).start()
 
         @pl.when(e // layers != core)

time: 211 us -> 211 us (level)
  no operation moved by 1% of the time
where the time goes in v4:
time: 211 us
  Pallas kernels  207 us (98%)
  local copies, waits for them, and re-layouts  3.32 us (2%)
    pallas_call x1, Pallas kernels, per_device(): pl.pallas_call(functools.partial(kernel, n_s, n_d, group, tile, rate), ou...  207 us

profile of v4, /device:TPU:8, one launch (start us, length us, event | category | flops | bytes accessed | tf_op | source)
XLA Modules:
  0.0 210.6 jit_solution(3220580534170427027)
XLA Ops:
  0.6 206.7 %shard_map.59 = (f32[1,4,128,512]{3,2,1,0:T(8,128)}, f32[1,4,128,512]{3,2,1,0:T(8,128)}) custom-call(bf16[768,512]{1,0:T(8,128)(2,1)} %bitcast.2, bf16[768,512]{1,0:T(8,128)(2,1)} %bitcast.3, bf16[1,4,128,512]{3,2,1,0:T(8,128)(2,1)} %w_in.1, bf16[1,4,128,512]{3,2,1,0:T(8,128)(2,1)} %w_out.1), custom_call_target="tpu_custom_call" | custom-call | flops 9663676416 | bytes 8388608 | tf_op jit(solution)/shard_map/pallas_call | solution.py:398
  207.3 0.0 copy-start
  207.3 2.4 %copy.8 = f32[1,4,128,512]{3,2,1,0:T(8,128)} copy(f32[1,4,128,512]{3,2,1,0:T(8,128)} %get-tuple-element.4) | data formatting | bytes 2097152
  209.7 0.0 copy-done
  209.7 1.0 copy.9
Async XLA Ops:
  207.3 2.4 %copy-start = (f32[1,4,128,512]{3,2,1,0:T(8,128)S(1)}, f32[1,4,128,512]{3,2,1,0:T(8,128)}, u32[]{:S(2)}) copy-start(f32[1,4,128,512]{3,2,1,0:T(8,128)} %get-tuple-element.5) | copy-start | bytes 3145732
